TPU v7x, 128 devices: a whole 4x4x4 slice. The times are simulated.
128 devices in a mesh: dp: 4 (over x), seq: 32 (over z, y, core).
Axes of the slice: x: 4, y: 4, z: 4, core: 2. Of those that a mesh axis runs over, the one named last changes fastest.
Arguments:
- ssm_input: bfloat16 [4, 8192, 3072], P('dp', 'seq'), may hold values from -6 to 6
- gate_input: bfloat16 [4, 8192, 3072], P('dp', 'seq'), may hold values from -6 to 6
- input_map: bfloat16 [4, 8192, 128], P('dp', 'seq'), may hold values from -0.52734375 to 0.52734375
- output_map: bfloat16 [4, 8192, 128], P('dp', 'seq'), may hold values from -6 to 6
- step_logit: bfloat16 [4, 8192, 48], P('dp', 'seq'), may hold values from -5 to 5
- step_bias: float32 [48], replicated, may hold values from -1 to 1
- decay_rate: float32 [48], replicated, may hold values from 6.1035156e-07 to 0.05
- skip_gain: float32 [48], replicated, may hold values from 0.5 to 1.5
- norm_gain: float32 [3072], replicated, may hold values from 0.1 to 1.9
- out_weight: bfloat16 [3072, 1536], replicated, may hold values from -0.109375 to 0.109375
- resets: int32 [4, 4], P('dp'), may hold values from 1 to 8191
- out_grad: bfloat16 [4, 8192, 1536], P('dp', 'seq'), may hold values from -6 to 6
Outputs:
- mixed_out: bfloat16 [4, 8192, 1536], P('dp', 'seq')
- grad_input: bfloat16 [4, 8192, 3072], P('dp', 'seq')
- grad_gate: bfloat16 [4, 8192, 3072], P('dp', 'seq')
- grad_inmap: bfloat16 [4, 8192, 128], P('dp', 'seq')
- grad_outmap: bfloat16 [4, 8192, 128], P('dp', 'seq')
- grad_step: bfloat16 [4, 8192, 48], P('dp', 'seq')
- grad_bias: float32 [48], replicated
- grad_rate: float32 [48], replicated
- grad_skip: float32 [48], replicated
- grad_gain: float32 [3072], replicated
- grad_weight: float32 [3072, 1536], P('seq')
All inputs are finite; a program needn't handle non-finite values.
Results may differ from a plain program's by a relative error of at most 0.0049.
Values sent between devices are 32-bit elements; how exact they have to be, the bound alone decides.
A program may use at most 384 MiB of HBM per device.

v0:
```python
import jax
import jax.numpy as jnp
from jax import lax
from jax.sharding import PartitionSpec as P

SPAN = 128
highest = lax.Precision.HIGHEST


def prefix(shard, axis, combine, identity, reverse):
    count, place = (lax.axis_size(axis), lax.axis_index(axis))
    everything = jax.tree.map(lambda part: lax.all_gather(part, axis), shard)
    start = jax.tree.map(
        lambda part, zero: jnp.broadcast_to(jnp.asarray(zero, part.dtype), part.shape),
        shard,
        identity,
    )

    def hop(k, before):
        at = count - 1 - k if reverse else k
        reached = at > place if reverse else at < place
        new = combine(before, jax.tree.map(lambda part: part[at], everything))
        return jax.tree.map(lambda a, b: jnp.where(reached, a, b), new, before)

    return lax.fori_loop(0, count, hop, start)


def block_step(state_in, inputs):
    x_blk, b_blk, c_blk, step_blk, decay_blk, flag_blk = inputs
    cumulative = jnp.cumsum(decay_blk, axis=0)
    counts = jnp.cumsum(flag_blk)
    block_len = flag_blk.shape[0]
    row_ids = lax.broadcasted_iota(jnp.int32, (block_len, block_len), 0)
    col_ids = lax.broadcasted_iota(jnp.int32, (block_len, block_len), 1)
    in_mask = ((row_ids >= col_ids) & (counts[:, None] == counts[None, :]))[:, :, None]
    gap_vals = cumulative[:, None, :] - cumulative[None, :, :]
    decay_mat = jnp.where(in_mask, jnp.exp(jnp.where(in_mask, gap_vals, 0.0)), 0.0)
    gram_mat = jnp.einsum("in,jn->ij", c_blk, b_blk, precision=highest)
    mixing = gram_mat[:, :, None] * decay_mat * step_blk[None, :, :]
    y_blk = jnp.einsum("ijh,jhp->ihp", mixing, x_blk, precision=highest)
    opened = (counts == 0)[:, None]
    from_start = jnp.where(opened, jnp.exp(jnp.where(opened, cumulative, 0.0)), 0.0)
    y_blk = y_blk + from_start[:, :, None] * jnp.einsum(
        "in,hpn->ihp", c_blk, state_in, precision=highest
    )
    keep_mask = (counts == counts[-1])[:, None]
    tail_weights = (
        jnp.where(
            keep_mask, jnp.exp(jnp.where(keep_mask, cumulative[-1][None, :] - cumulative, 0.0)), 0.0
        )
        * step_blk
    )
    whole_decay = jnp.where(counts[-1] == 0, jnp.exp(cumulative[-1]), 0.0)
    new_state = whole_decay[:, None, None] * state_in + jnp.einsum(
        "jhp,jn->hpn", tail_weights[:, :, None] * x_blk, b_blk, precision=highest
    )
    return (new_state, y_blk)


def ssd_blocks(x_heads, b_float, c_float, step_vals, log_decay, flags, state_in):
    num_blocks = x_heads.shape[0] // SPAN

    def to_blocks(values):
        return values.reshape((num_blocks, SPAN) + values.shape[1:])

    final_state, y_blocks = lax.scan(
        block_step,
        state_in,
        (
            to_blocks(x_heads),
            to_blocks(b_float),
            to_blocks(c_float),
            to_blocks(step_vals),
            to_blocks(log_decay),
            to_blocks(flags),
        ),
    )
    return (final_state, y_blocks.reshape(x_heads.shape))


def gate_norm(y_ssd, x_float, z_float, skip_gain, norm_gain):
    num_heads = skip_gain.shape[0]
    rows_here = x_float.shape[0]
    y_full = y_ssd.reshape(rows_here, -1) + (
        x_float.reshape(rows_here, num_heads, -1) * skip_gain[None, :, None]
    ).reshape(x_float.shape)
    gated_vals = y_full * jax.nn.silu(z_float)
    scale_inv = lax.rsqrt(jnp.mean(gated_vals * gated_vals, axis=-1, keepdims=True) + 1e-05)
    return gated_vals * scale_inv * norm_gain


def step_sizes(logit_vals, bias_in, rate_in):
    step_vals = jax.nn.softplus(logit_vals + bias_in)
    return (step_vals, -rate_in * step_vals)


def combine(earlier, later):
    return (earlier[0] * later[0], later[0][:, None, None] * earlier[1] + later[1])


def per_device(
    ssm_input,
    gate_input,
    input_map,
    output_map,
    step_logit,
    step_bias,
    decay_rate,
    skip_gain,
    norm_gain,
    out_weight,
    resets,
    out_grad,
):
    rows_here = ssm_input.shape[1]
    num_heads = step_bias.shape[0]
    x_float = ssm_input[0].astype(jnp.float32)
    z_float = gate_input[0].astype(jnp.float32)
    b_float = input_map[0].astype(jnp.float32)
    c_float = output_map[0].astype(jnp.float32)
    logit_float = step_logit[0].astype(jnp.float32)
    inner_width = x_float.shape[1]
    head_size = inner_width // num_heads
    x_heads = x_float.reshape(rows_here, num_heads, head_size)
    positions = lax.axis_index("seq") * rows_here + lax.iota(jnp.int32, rows_here)
    flags = jnp.max((positions[:, None] == resets[0][None, :]).astype(jnp.int32), axis=1)
    counts = jnp.cumsum(flags)
    opened = (counts == 0)[:, None]
    clean_shard = counts[-1] == 0
    empty_state = jnp.zeros((num_heads, head_size, b_float.shape[1]), jnp.float32)
    identity = (jnp.ones((num_heads,), jnp.float32), empty_state)
    step_vals, log_decay = step_sizes(logit_float, step_bias, decay_rate)
    cumulative = jnp.cumsum(log_decay, axis=0)
    from_start = jnp.where(opened, jnp.exp(jnp.where(opened, cumulative, 0.0)), 0.0)
    shard_through = jnp.where(clean_shard, jnp.exp(cumulative[-1]), 0.0)
    step_vals, cumulative, from_start, through = (step_vals, cumulative, from_start, shard_through)
    keep_mask = (counts == counts[-1])[:, None]
    tail_weights = (
        jnp.where(
            keep_mask, jnp.exp(jnp.where(keep_mask, cumulative[-1][None, :] - cumulative, 0.0)), 0.0
        )
        * step_vals
    )
    shard_state = jnp.einsum(
        "thp,tn->hpn", tail_weights[:, :, None] * x_heads, b_float, precision=highest
    )
    incoming = prefix((through, shard_state), "seq", combine, identity, False)[1]

    def from_incoming(x_part, b_part, c_part, logit_vals, bias_in, rate_in):
        step_part, decay_part = step_sizes(logit_vals, bias_in, rate_in)
        return ssd_blocks(x_part, b_part, c_part, step_part, decay_part, flags, incoming)

    (final_state, y_ssd), ssd_pullback = jax.vjp(
        from_incoming, x_heads, b_float, c_float, logit_float, step_bias, decay_rate
    )
    normed_f, post_pullback = jax.vjp(gate_norm, y_ssd, x_float, z_float, skip_gain, norm_gain)
    normed = normed_f.astype(jnp.bfloat16)
    mixed = jnp.dot(normed, out_weight, preferred_element_type=jnp.float32).astype(jnp.bfloat16)
    grad_rows = out_grad[0]
    normed_grad = lax.dot_general(
        grad_rows, out_weight, (((1,), (1,)), ((), ())), preferred_element_type=jnp.float32
    )
    y_grad, x_grad_skip, z_grad, skip_grad, gain_grad = post_pullback(normed_grad)
    start_grad = jnp.einsum(
        "thp,tn->hpn", from_start[:, :, None] * y_grad, c_float, precision=highest
    )
    later_grad = prefix((through, start_grad), "seq", combine, identity, True)[1]
    x_grad, b_grad, c_grad, logit_grad, bias_grad, rate_grad = ssd_pullback((later_grad, y_grad))
    bias_sum, rate_sum, skip_sum, gain_sum = lax.psum(
        (bias_grad, rate_grad, skip_grad, gain_grad), ("dp", "seq")
    )
    seq_rows = lax.psum_scatter(
        lax.dot_general(
            normed, grad_rows, (((0,), (0,)), ((), ())), preferred_element_type=jnp.float32
        ),
        "seq",
        scatter_dimension=0,
        tiled=True,
    )
    weight_grad = lax.psum(seq_rows, "dp")
    grad_input = (x_grad.reshape(rows_here, inner_width) + x_grad_skip).astype(jnp.bfloat16)
    return (
        mixed[None],
        grad_input[None],
        z_grad.astype(jnp.bfloat16)[None],
        b_grad.astype(jnp.bfloat16)[None],
        c_grad.astype(jnp.bfloat16)[None],
        logit_grad.astype(jnp.bfloat16)[None],
        bias_sum,
        rate_sum,
        skip_sum,
        gain_sum,
        weight_grad,
    )


def solution(mesh):
    placed = (
        P("dp", "seq", None),
        P("dp", "seq", None),
        P("dp", "seq", None),
        P("dp", "seq", None),
        P("dp", "seq", None),
        P(),
        P(),
        P(),
        P(),
        P(),
        P("dp", None),
        P("dp", "seq", None),
    )
    return jax.shard_map(
        per_device,
        mesh=mesh,
        in_specs=placed,
        out_specs=(
            P("dp", "seq", None),
            P("dp", "seq", None),
            P("dp", "seq", None),
            P("dp", "seq", None),
            P("dp", "seq", None),
            P("dp", "seq", None),
            P(),
            P(),
            P(),
            P(),
            P("seq", None),
        ),
        check_vma=False,
    )
```

profile of v0, /device:TPU:1, one launch (start us, length us, event | category | flops | bytes accessed | tf_op | source)
XLA Modules:
  0.0 973.6 jit_solution(15452090480564412764)
XLA Ops:
  55.9 24.0 %all-gather.2 = f32[32,1,48]{2,1,0:T(1,128)S(1)} all-gather(f32[1,1,48]{2,1,0:T(1,128)S(1)} %bitcast.581), channel_id=1, replica_groups=mesh['dp'=4,'seq'=32] {'seq'}, dimensions={0}, use_global_device_ids=true | all-gather | bytes 6336 | tf_op jit(solution)/shard_map/all_gather | solution.py:12
  79.9 115.2 %all-gather.6.cloned.1.call-done = f32[1536,64,128]{2,1,0:T(8,128)} async-done(((f32[48,64,128]{2,1,0:T(8,128)}), f32[1536,64,128]{2,1,0:T(8,128)}) %all-gather.6.cloned.1.call-update) | async-done | bytes 50331664 | tf_op jit(solution)/shard_map/all_gather | solution.py:12
  195.1 58.0 %while.116 = (s32[]{:T(128)}, f32[48,64,128]{2,1,0:T(8,128)S(1)}, s32[]{:T(128)}, f32[32,48]{1,0:T(8,128)S(1)}, f32[32,48,64,128]{3,2,1,0:T(8,128)}, /*index=5*/s32[]{:T(128)}, s32[]{:T(128)}) while((s32[]{:T(128)}, f32[48,64,128]{2,1,0:T(8,128)S(1)}, s32[]{:T(128)}, f32[32,48]{1,0:T(8,128)S(1)}, f32[32,48,64,128]{3,2,1,0:T(8,128)}, ...), condition=%wide.region_6.7_spmd.clone, body=%wide.region_5.6_spmd.clone.sunk | while | flops 1572868 | bytes 4719273 | solution.py:25
  259.2 154.5 %while.115 = (s32[]{:T(128)}, f32[48,64,128]{2,1,0:T(8,128)S(1)}, f32[2,128,48,64]{1,3,2,0:T(8,128)}, pred[2,128,128,48]{2,1,3,0:T(32,128)(4,1)}, f32[2,128,128,...) while((s32[]{:T(128)}, f32[48,64,128]{2,1,0:T(8,128)S(1)}, ...), condition=%wide.region_10.11_spmd.clone, body=%wide.region_7.10_spmd.clone.sunk | while | flops 1848273152 | bytes 111490832 | solution.py:66
  262.9 11.3 %broadcast_multiply_fusion.4 = (f32[1,128,128,48]{3,2,1,0:T(8,128)}, f32[1,128,128,48]{3,2,1,0:T(8,128)}, f32[1,128,128,48]{3,2,1,0:T(8,128)}, f32[1,128,128,48]{3,2,1,0:T(8,128)}) fusion(f32[128,48]{1,0:T(8,128)S(1)} %get-tuple-element.2450, f32[128,48]{1,0:T(8,128)S(1)} %reduce_window_sum.92, pred[128,128]{1,0:T(8,128)(4,1)S(1)} %fusion.251, ...), kind=kLoop, calls=%fused_computation.99.clone.1 | loop fusion | flops 3932160 | bytes 12713984 | tf_op jit(solution)/shard_map/jvp()/while/body/eval_jaxpr/mul | solution.py:39
  274.2 6.9 copy.272
  281.1 6.8 copy.273
  294.2 6.9 copy.269
  301.1 6.8 copy.270
  307.9 6.4 constant_dynamic-update-slice_fusion.21
  317.1 7.6 bitcast_dynamic-update-slice_fusion.13
  339.9 11.3 %broadcast_multiply_fusion.4 = (f32[1,128,128,48]{3,2,1,0:T(8,128)}, f32[1,128,128,48]{3,2,1,0:T(8,128)}, f32[1,128,128,48]{3,2,1,0:T(8,128)}, f32[1,128,128,48]{3,2,1,0:T(8,128)}) fusion(f32[128,48]{1,0:T(8,128)S(1)} %get-tuple-element.2450, f32[128,48]{1,0:T(8,128)S(1)} %reduce_window_sum.92, pred[128,128]{1,0:T(8,128)(4,1)S(1)} %fusion.251, ...), kind=kLoop, calls=%fused_computation.99.clone.1 | loop fusion | flops 3932160 | bytes 12713984 | tf_op jit(solution)/shard_map/jvp()/while/body/eval_jaxpr/mul | solution.py:39
  351.2 6.9 copy.272
  358.1 6.8 copy.273
  371.2 6.9 copy.269
  378.1 6.8 copy.270
  384.9 6.4 constant_dynamic-update-slice_fusion.21
  394.2 7.6 bitcast_dynamic-update-slice_fusion.13
  413.7 7.7 multiply_reduce_fusion.2
  425.3 7.8 fusion.146
  439.6 6.5 copy.180
  446.1 6.4 reshape.1022
  452.5 10.8 %multiply_reduce_fusion = (f32[3072]{0:T(1024)}, f32[256]{0:T(256)S(1)}, f32[256,3072]{1,0:T(8,128)S(1)}) fusion(f32[256]{0:T(256)S(1)} %bitcast_rsqrt_fusion, bf16[1,256,3072]{2,1,0:T(8,128)(2,1)} %param.21, f32[256,3072]{1,0:T(8,128)} %reshape.1022, f32[3072]{0:T(1024)S(1)} %mul.708, bf16[1,256,3072]{2,1,0:T(8,128)(2,1)S(1)} %copy-done.8, ...), kind=kOutput, calls=%fused_computation.207 | convolution fusion | flops 2427712256 | bytes 19699712 | tf_op jit(solution)/shard_map/dot_general | solution.py:160
  486.6 7.1 copy.158
  494.4 10.0 %fusion.143 = bf16[1,256,1536]{2,1,0:T(8,128)(2,1)} fusion(bf16[3072,1536]{1,0:T(8,128)(2,1)} %param.29, f32[3072]{0:T(1024)S(1)} %copy-done.27, f32[256]{0:T(256)S(1)} %bitcast_rsqrt_fusion, f32[256,3072]{1,0:T(8,128)} %reshape.1022, bf16[1,256,3072]{2,1,0:T(8,128)(2,1)} %param.20, f32[3072]{0:T(1024)S(1)} %mul.708, bf16[1,256,3072]{2,1,0:T(8,128)(2,1)} %param.21), kind=kOutput, calls=%fused_computation.213 | convolution fusion | flops 2425749504 | bytes 16540672 | tf_op jit(solution)/shard_map/dot_general | solution.py:158
  504.3 48.3 %reduce-scatter.2.cloned.1.call-done = f32[96,1536]{1,0:T(8,128)} async-done(((f32[3072,1536]{1,0:T(8,128)}), f32[96,1536]{1,0:T(8,128)}) %reduce-scatter.2.cloned.1.call-update) | async-done | bytes 589840 | tf_op jit(solution)/shard_map/reduce_scatter | solution.py:172
  552.7 161.2 %all-gather.8.cloned.1.call-done = f32[1536,64,128]{2,1,0:T(8,128)} async-done(((f32[48,64,128]{2,1,0:T(8,128)}), f32[1536,64,128]{2,1,0:T(8,128)}) %all-gather.8.cloned.1.call-update) | async-done | bytes 50331664 | tf_op jit(solution)/shard_map/all_gather | solution.py:12
  713.8 79.9 %while.117 = (s32[]{:T(128)}, f32[48,64,128]{2,1,0:T(8,128)S(1)}, s32[]{:T(128)}, f32[32,48]{1,0:T(8,128)}, f32[32,48,64,128]{3,2,1,0:T(8,128)}, /*index=5*/s32[]{:T(128)}, s32[]{:T(128)}, s32[]{:T(128)}, s32[]{:T(128)}) while((s32[]{:T(128)}, f32[48,64,128]{2,1,0:T(8,128)S(1)}, s32[]{:T(128)}, f32[32,48]{1,0:T(8,128)}, ...), condition=%wide.region_14.15_spmd.clone, body=%wide.region_13.14_spmd.clone.sunk | while | flops 1572872 | bytes 4719335 | solution.py:25
  797.9 83.0 %while.114 = (s32[]{:T(128)}, f32[48,64,128]{2,1,0:T(8,128)S(1)}, f32[2,128,48,64]{1,3,2,0:T(8,128)}, bf16[2,128,128]{2,1,0:T(8,128)(2,1)}, bf16[2,128,128]{2,1,...) while((s32[]{:T(128)}, f32[48,64,128]{2,1,0:T(8,128)S(1)}, ...), condition=%wide.region_25.26_spmd, body=%wide.region_15.25_spmd.sunk | while | flops 3688450048 | bytes 77251128 | solution.py:66
  798.9 11.1 %fusion.235 = (f32[128,48]{0,1:T(8,128)S(1)}, f32[128,48]{0,1:T(8,128)S(1)}, f32[128,128]{1,0:T(8,128)S(1)}, f32[128,48]{0,1:T(8,128)S(1)}) fusion(f32[2,128,128,48]{2,1,3,0:T(8,128)} %get-tuple-element.2728, s32[]{:T(128)S(6)} %sub.274, f32[128,48]{0,1:T(8,128)S(1)} %dynamic-slice_bitcast_fusion.18, ...), kind=kOutput, calls=%fused_computation.91.clone.1 | convolution fusion | flops 612595712 | bytes 13600256 | tf_op jit(solution)/shard_map/transpose(jvp())/while/body/eval_jaxpr/ijh,jhp->ihp/dot_general | solution.py:40
  840.2 11.1 %fusion.235 = (f32[128,48]{0,1:T(8,128)S(1)}, f32[128,48]{0,1:T(8,128)S(1)}, f32[128,128]{1,0:T(8,128)S(1)}, f32[128,48]{0,1:T(8,128)S(1)}) fusion(f32[2,128,128,48]{2,1,3,0:T(8,128)} %get-tuple-element.2728, s32[]{:T(128)S(6)} %sub.274, f32[128,48]{0,1:T(8,128)S(1)} %dynamic-slice_bitcast_fusion.18, ...), kind=kOutput, calls=%fused_computation.91.clone.1 | convolution fusion | flops 612595712 | bytes 13600256 | tf_op jit(solution)/shard_map/transpose(jvp())/while/body/eval_jaxpr/ijh,jhp->ihp/dot_general | solution.py:40
  895.7 64.7 %all-reduce.2 = (f32[48]{0:T(128)}, f32[48]{0:T(128)}, f32[48]{0:T(128)}, f32[3072]{0:T(1024)}) all-reduce(f32[48]{0:T(128)S(1)} %get-tuple-element.1778, f32[48]{0:T(128)S(1)} %neg.49, f32[48]{0:T(128)S(1)} %copy-done.36, f32[3072]{0:T(1024)S(1)} %copy-done.32), channel_id=1, replica_groups=mesh['dp'=4,'seq'=32] {'dp','seq'}, use_global_device_ids=true, to_apply=%region_27.28 | all-reduce | flops 3216 | bytes 25728 | tf_op jit(solution)/shard_map/psum | solution.py:169
  (481 shorter events, 356.5 us)
Async XLA Ops:
  7.2 418.2 %copy-start = (bf16[1,256,1536]{2,1,0:T(8,128)(2,1)S(1)}, bf16[1,256,1536]{2,1,0:T(8,128)(2,1)}, u32[]{:S(2)}) copy-start(bf16[1,256,1536]{2,1,0:T(8,128)(2,1)} %param.31) | copy-start | bytes 2359300
  7.2 187.9 %all-gather.6.cloned.1.call-start = ((), (), s32[]{:S(2)}) async-start(), calls=%async_computation.3 | async-start | bytes 51904512 | tf_op jit(solution)/shard_map/all_gather | solution.py:12
  12.5 67.4 %copy-start.33 = (f32[48]{0:T(128)}, f32[48]{0:T(128)S(1)}, u32[]{:S(2)}) copy-start(f32[48]{0:T(128)S(1)} %neg.43) | copy-start | bytes 580
  33.8 518.9 %reduce-scatter.2.cloned.1.call-start = ((), (), s32[]{:S(2)}) async-start(), calls=%async_computation.1 | async-start | bytes 19464192 | tf_op jit(solution)/shard_map/reduce_scatter | solution.py:172
  33.9 45.9 %copy-start.12 = (f32[1,256,48]{2,1,0:T(8,128)}, f32[1,256,48]{2,1,0:T(8,128)S(1)}, u32[]{:S(2)}) copy-start(f32[1,256,48]{2,1,0:T(8,128)S(1)} %copy.179) | copy-start | bytes 147460
  49.7 5.5 copy-start.26
  49.7 30.2 %copy-start.29 = (f32[48]{0:T(128)S(1)}, f32[48]{0:T(128)}, u32[]{:S(2)}) copy-start(f32[48]{0:T(128)} %param.25) | copy-start | bytes 580
  330.8 4.9 copy-start.43
  413.7 7.7 copy-start.20
  433.2 280.7 %all-gather.8.cloned.1.call-start = ((), (), s32[]{:S(2)}) async-start(), calls=%async_computation.4 | async-start | bytes 51904512 | tf_op jit(solution)/shard_map/all_gather | solution.py:12
  446.1 6.4 copy-start.8
  446.1 6.4 copy-start.27
  452.5 10.8 %copy-start.10 = (f32[256,3072]{1,0:T(8,128)S(1)}, f32[256,3072]{1,0:T(8,128)}, u32[]{:S(2)}) copy-start(f32[256,3072]{1,0:T(8,128)} %reshape.1022) | copy-start | bytes 9437188
  452.5 10.8 %copy-start.11 = (bf16[1,256,3072]{2,1,0:T(8,128)(2,1)S(1)}, bf16[1,256,3072]{2,1,0:T(8,128)(2,1)}, u32[]{:S(2)}) copy-start(bf16[1,256,3072]{2,1,0:T(8,128)(2,1)} %param.21) | copy-start | bytes 4718596
  463.3 5.6 copy-start.9
  479.8 485.2 %all-reduce.5.cloned.1.call-start = ((), (), s32[]{:S(2)}) async-start(), calls=%async_computation.2 | async-start | bytes 1179648 | tf_op jit(solution)/shard_map/psum | solution.py:180
  797.9 84.8 %copy-start.13 = (f32[1,256,48]{2,1,0:T(8,128)S(1)}, f32[1,256,48]{2,1,0:T(8,128)}, u32[]{:S(2)}) copy-start(f32[1,256,48]{2,1,0:T(8,128)} %copy-done.12) | copy-start | bytes 147460
  797.9 84.8 %copy-start.30 = (f32[48]{0:T(128)S(1)}, f32[48]{0:T(128)}, u32[]{:S(2)}) copy-start(f32[48]{0:T(128)} %param.25) | copy-start | bytes 580
  797.9 84.8 %copy-start.34 = (f32[48]{0:T(128)S(1)}, f32[48]{0:T(128)}, u32[]{:S(2)}) copy-start(f32[48]{0:T(128)} %copy-done.33) | copy-start | bytes 580
  798.9 11.2 %copy-start.5 = (f32[2,48,64,128]{3,2,1,0:T(8,128)S(1)}, f32[2,48,64,128]{3,2,1,0:T(8,128)}, u32[]{:S(2)}) copy-start(f32[2,48,64,128]{3,2,1,0:T(8,128)} %get-tuple-element.2715) | copy-start | bytes 9437188 | tf_op jit(solution)/shard_map/transpose(jvp())/while
  821.9 9.6 copy-start.24
  821.9 9.9 %copy-start.1 = (f32[2,128,48,64]{1,3,2,0:T(8,128)S(1)}, f32[2,128,48,64]{1,3,2,0:T(8,128)}, u32[]{:S(2)}) copy-start(f32[2,128,48,64]{1,3,2,0:T(8,128)} %get-tuple-element.2706) | copy-start | bytes 9437188 | tf_op jit(solution)/shard_map/transpose(jvp())/while
  821.9 9.9 %copy-start.4 = (f32[128,48,64]{0,2,1:T(8,128)S(1)}, f32[128,48,64]{0,2,1:T(8,128)}, u32[]{:S(2)}) copy-start(f32[128,48,64]{0,2,1:T(8,128)} %get-tuple-element.2407) | copy-start | bytes 4718596 | tf_op jit(solution)/shard_map/transpose(jvp())/while
  831.8 5.5 copy-start.25
  840.2 11.2 %copy-start.5 = (f32[2,48,64,128]{3,2,1,0:T(8,128)S(1)}, f32[2,48,64,128]{3,2,1,0:T(8,128)}, u32[]{:S(2)}) copy-start(f32[2,48,64,128]{3,2,1,0:T(8,128)} %get-tuple-element.2715) | copy-start | bytes 9437188 | tf_op jit(solution)/shard_map/transpose(jvp())/while
  863.2 9.6 copy-start.24
  863.2 9.9 %copy-start.1 = (f32[2,128,48,64]{1,3,2,0:T(8,128)S(1)}, f32[2,128,48,64]{1,3,2,0:T(8,128)}, u32[]{:S(2)}) copy-start(f32[2,128,48,64]{1,3,2,0:T(8,128)} %get-tuple-element.2706) | copy-start | bytes 9437188 | tf_op jit(solution)/shard_map/transpose(jvp())/while
  863.2 9.9 %copy-start.4 = (f32[128,48,64]{0,2,1:T(8,128)S(1)}, f32[128,48,64]{0,2,1:T(8,128)}, u32[]{:S(2)}) copy-start(f32[128,48,64]{0,2,1:T(8,128)} %get-tuple-element.2407) | copy-start | bytes 4718596 | tf_op jit(solution)/shard_map/transpose(jvp())/while
  873.1 5.4 copy-start.25
  889.1 5.9 copy-start.15
  889.1 6.6 copy-start.32
  889.1 6.6 copy-start.36
  (34 other events, 101.2 us)
Sparse Core Ops, SparseCore 0:
  33.9 161.1 all-gather.5
  433.3 119.3 reduce-scatter.1
  555.8 158.0 all-gather.7
  716.2 40.1 all-reduce.4
where the time goes:
time: 984 us; the launch traced here: 974 us
  waiting for transfers between devices  325 us (33%)
  local copies, waits for them, and re-layouts  220 us (22%)
  other arithmetic  192 us (20%)
  matrix products  128 us (13%)
  blocking collectives  88.7 us (9%)
  between operations  15.1 us (2%)
    all_gather x2, waiting for transfers between devices, prefix(): everything = jax.tree.map(lambda part: lax.all_gather(part, axis), shard)  276 us
    select_n x64, other arithmetic, hop(): return jax.tree.map(lambda a, b: jnp.where(reached, a, b), new, before)  113 us
    dynamic_update_slice x44, local copies, waits for them, and re-layouts, ssd_blocks(): lax.scan(block_step, state_in, (to_blocks(x_heads), to_blocks(b_float), t...  89 us
    psum x1, blocking collectives, per_device(): lax.psum((bias_grad, rate_grad, skip_grad, gain_grad), ('dp', 'seq'))  64.7 us
    reduce_scatter x1, waiting for transfers between devices, per_device(): lax.psum_scatter(lax.dot_general(normed, grad_rows, (((0,), (0,)), ((), (...  48.3 us
    dot_general x6, matrix products, block_step(): y_blk = jnp.einsum('ijh,jhp->ihp', mixing, x_blk, precision=highest)  48.3 us
    all_gather x1, blocking collectives, prefix(): everything = jax.tree.map(lambda part: lax.all_gather(part, axis), shard)  24 us
    mul x2, other arithmetic, block_step(): mixing = gram_mat[:, :, None] * decay_mat * step_blk[None, :, :]  22.6 us
  transfers between devices with their start and end apart: 4, of which 3 were waited for; matrix products, arithmetic and copies ran while one was open for 28% of the time, Pallas kernels for 0%

commit v1 on v0

--- a/solution.py
+++ b/solution.py
@@ -167,7 +167,7 @@
     later_grad = prefix((through, start_grad), "seq", combine, identity, True)[1]
     x_grad, b_grad, c_grad, logit_grad, bias_grad, rate_grad = ssd_pullback((later_grad, y_grad))
     bias_sum, rate_sum, skip_sum, gain_sum = lax.psum(
-        (bias_grad, rate_grad, skip_grad, gain_grad), ("dp", "seq")
+        lax.psum((bias_grad, rate_grad, skip_grad, gain_grad), "seq"), "dp"
     )
     seq_rows = lax.psum_scatter(
         lax.dot_general(

time: 984 us -> 1060 us (1.077)
  blocking collectives: 88.7 us -> 159 us
    psum x1 -> x2, blocking collectives: 64.7 us -> 135 us  [the longest x1 121 us: per_device(): lax.psum((bias_grad, rate_grad, skip_grad, gain_grad), 'seq')]
  transfers between devices with their start and end apart: 4 -> 4, of which waited for: 3 -> 3; matrix products, arithmetic and copies ran while one was open for 28% -> 26% of each run, Pallas kernels for 0% -> 0%
where the time goes in v1:
time: 1060 us; the launch traced here: 1040 us
  waiting for transfers between devices  325 us (31%)
  local copies, waits for them, and re-layouts  220 us (21%)
  other arithmetic  192 us (18%)
  blocking collectives  159 us (15%)
  matrix products  128 us (12%)
  between operations  15.1 us (1%)
    all_gather x2, waiting for transfers between devices, prefix(): everything = jax.tree.map(lambda part: lax.all_gather(part, axis), shard)  276 us
    psum x1, blocking collectives, per_device(): lax.psum((bias_grad, rate_grad, skip_grad, gain_grad), 'seq')  121 us
    select_n x64, other arithmetic, hop(): return jax.tree.map(lambda a, b: jnp.where(reached, a, b), new, before)  113 us
    dynamic_update_slice x44, local copies, waits for them, and re-layouts, ssd_blocks(): lax.scan(block_step, state_in, (to_blocks(x_heads), to_blocks(b_float), t...  89 us
    reduce_scatter x1, waiting for transfers between devices, per_device(): lax.psum_scatter(lax.dot_general(normed, grad_rows, (((0,), (0,)), ((), (...  48.3 us
    dot_general x6, matrix products, block_step(): y_blk = jnp.einsum('ijh,jhp->ihp', mixing, x_blk, precision=highest)  48.3 us
    all_gather x1, blocking collectives, prefix(): everything = jax.tree.map(lambda part: lax.all_gather(part, axis), shard)  24 us
    mul x2, other arithmetic, block_step(): mixing = gram_mat[:, :, None] * decay_mat * step_blk[None, :, :]  22.6 us
  transfers between devices with their start and end apart: 4, of which 3 were waited for; matrix products, arithmetic and copies ran while one was open for 26% of the time, Pallas kernels for 0%

profile of v1, /device:TPU:1, one launch (start us, length us, event | category | flops | bytes accessed | tf_op | source)
XLA Modules:
  0.0 1044.0 jit_solution(5416981111853856829)
XLA Ops:
  55.9 24.0 %all-gather.2 = f32[32,1,48]{2,1,0:T(1,128)S(1)} all-gather(f32[1,1,48]{2,1,0:T(1,128)S(1)} %bitcast.581), channel_id=1, replica_groups=mesh['dp'=4,'seq'=32] {'seq'}, dimensions={0}, use_global_device_ids=true | all-gather | bytes 6336 | tf_op jit(solution)/shard_map/all_gather | solution.py:12
  79.9 115.2 %all-gather.6.cloned.1.call-done = f32[1536,64,128]{2,1,0:T(8,128)} async-done(((f32[48,64,128]{2,1,0:T(8,128)}), f32[1536,64,128]{2,1,0:T(8,128)}) %all-gather.6.cloned.1.call-update) | async-done | bytes 50331664 | tf_op jit(solution)/shard_map/all_gather | solution.py:12
  195.1 58.0 %while.116 = (s32[]{:T(128)}, f32[48,64,128]{2,1,0:T(8,128)S(1)}, s32[]{:T(128)}, f32[32,48]{1,0:T(8,128)S(1)}, f32[32,48,64,128]{3,2,1,0:T(8,128)}, /*index=5*/s32[]{:T(128)}, s32[]{:T(128)}) while((s32[]{:T(128)}, f32[48,64,128]{2,1,0:T(8,128)S(1)}, s32[]{:T(128)}, f32[32,48]{1,0:T(8,128)S(1)}, f32[32,48,64,128]{3,2,1,0:T(8,128)}, ...), condition=%wide.region_6.7_spmd.clone, body=%wide.region_5.6_spmd.clone.sunk | while | flops 1572868 | bytes 4719273 | solution.py:25
  259.2 154.5 %while.115 = (s32[]{:T(128)}, f32[48,64,128]{2,1,0:T(8,128)S(1)}, f32[2,128,48,64]{1,3,2,0:T(8,128)}, pred[2,128,128,48]{2,1,3,0:T(32,128)(4,1)}, f32[2,128,128,...) while((s32[]{:T(128)}, f32[48,64,128]{2,1,0:T(8,128)S(1)}, ...), condition=%wide.region_10.11_spmd.clone, body=%wide.region_7.10_spmd.clone.sunk | while | flops 1848273152 | bytes 111490832 | solution.py:66
  262.9 11.3 %broadcast_multiply_fusion.4 = (f32[1,128,128,48]{3,2,1,0:T(8,128)}, f32[1,128,128,48]{3,2,1,0:T(8,128)}, f32[1,128,128,48]{3,2,1,0:T(8,128)}, f32[1,128,128,48]{3,2,1,0:T(8,128)}) fusion(f32[128,48]{1,0:T(8,128)S(1)} %get-tuple-element.2454, f32[128,48]{1,0:T(8,128)S(1)} %reduce_window_sum.92, pred[128,128]{1,0:T(8,128)(4,1)S(1)} %fusion.251, ...), kind=kLoop, calls=%fused_computation.99.clone.1 | loop fusion | flops 3932160 | bytes 12713984 | tf_op jit(solution)/shard_map/jvp()/while/body/eval_jaxpr/mul | solution.py:39
  274.2 6.9 copy.272
  281.1 6.8 copy.273
  294.2 6.9 copy.269
  301.1 6.8 copy.270
  307.9 6.4 constant_dynamic-update-slice_fusion.21
  317.1 7.6 bitcast_dynamic-update-slice_fusion.13
  339.9 11.3 %broadcast_multiply_fusion.4 = (f32[1,128,128,48]{3,2,1,0:T(8,128)}, f32[1,128,128,48]{3,2,1,0:T(8,128)}, f32[1,128,128,48]{3,2,1,0:T(8,128)}, f32[1,128,128,48]{3,2,1,0:T(8,128)}) fusion(f32[128,48]{1,0:T(8,128)S(1)} %get-tuple-element.2454, f32[128,48]{1,0:T(8,128)S(1)} %reduce_window_sum.92, pred[128,128]{1,0:T(8,128)(4,1)S(1)} %fusion.251, ...), kind=kLoop, calls=%fused_computation.99.clone.1 | loop fusion | flops 3932160 | bytes 12713984 | tf_op jit(solution)/shard_map/jvp()/while/body/eval_jaxpr/mul | solution.py:39
  351.2 6.9 copy.272
  358.1 6.8 copy.273
  371.2 6.9 copy.269
  378.1 6.8 copy.270
  384.9 6.4 constant_dynamic-update-slice_fusion.21
  394.2 7.6 bitcast_dynamic-update-slice_fusion.13
  413.7 7.7 multiply_reduce_fusion.2
  425.3 7.8 fusion.146
  439.6 6.5 copy.180
  452.5 10.8 %multiply_reduce_fusion = (f32[3072]{0:T(1024)}, f32[256]{0:T(256)S(1)}, f32[256,3072]{1,0:T(8,128)S(1)}) fusion(f32[256]{0:T(256)S(1)} %bitcast_rsqrt_fusion, bf16[1,256,3072]{2,1,0:T(8,128)(2,1)} %param.21, f32[256,3072]{1,0:T(8,128)} %reshape.1022, f32[3072]{0:T(1024)S(1)} %mul.708, bf16[1,256,3072]{2,1,0:T(8,128)(2,1)S(1)} %copy-done.8, ...), kind=kOutput, calls=%fused_computation.207 | convolution fusion | flops 2427712256 | bytes 19699712 | tf_op jit(solution)/shard_map/dot_general | solution.py:160
  486.6 7.1 copy.158
  494.4 10.0 fusion.143
  504.3 48.3 %reduce-scatter.2.cloned.1.call-done = f32[96,1536]{1,0:T(8,128)} async-done(((f32[3072,1536]{1,0:T(8,128)}), f32[96,1536]{1,0:T(8,128)}) %reduce-scatter.2.cloned.1.call-update) | async-done | bytes 589840 | tf_op jit(solution)/shard_map/reduce_scatter | solution.py:172
  552.7 161.2 %all-gather.8.cloned.1.call-done = f32[1536,64,128]{2,1,0:T(8,128)} async-done(((f32[48,64,128]{2,1,0:T(8,128)}), f32[1536,64,128]{2,1,0:T(8,128)}) %all-gather.8.cloned.1.call-update) | async-done | bytes 50331664 | tf_op jit(solution)/shard_map/all_gather | solution.py:12
  713.8 79.9 %while.117 = (s32[]{:T(128)}, f32[48,64,128]{2,1,0:T(8,128)S(1)}, s32[]{:T(128)}, f32[32,48]{1,0:T(8,128)}, f32[32,48,64,128]{3,2,1,0:T(8,128)}, /*index=5*/s32[]{:T(128)}, s32[]{:T(128)}, s32[]{:T(128)}, s32[]{:T(128)}) while((s32[]{:T(128)}, f32[48,64,128]{2,1,0:T(8,128)S(1)}, s32[]{:T(128)}, f32[32,48]{1,0:T(8,128)}, ...), condition=%wide.region_14.15_spmd.clone, body=%wide.region_13.14_spmd.clone.sunk | while | flops 1572872 | bytes 4719335 | solution.py:25
  797.9 83.0 %while.114 = (s32[]{:T(128)}, f32[48,64,128]{2,1,0:T(8,128)S(1)}, f32[2,128,48,64]{1,3,2,0:T(8,128)}, bf16[2,128,128]{2,1,0:T(8,128)(2,1)}, bf16[2,128,128]{2,1,...) while((s32[]{:T(128)}, f32[48,64,128]{2,1,0:T(8,128)S(1)}, ...), condition=%wide.region_25.26_spmd, body=%wide.region_15.25_spmd.sunk | while | flops 3688450048 | bytes 77251128 | solution.py:66
  798.9 11.1 %fusion.235 = (f32[128,48]{0,1:T(8,128)S(1)}, f32[128,48]{0,1:T(8,128)S(1)}, f32[128,128]{1,0:T(8,128)S(1)}, f32[128,48]{0,1:T(8,128)S(1)}) fusion(f32[2,128,128,48]{2,1,3,0:T(8,128)} %get-tuple-element.2732, s32[]{:T(128)S(6)} %sub.274, f32[128,48]{0,1:T(8,128)S(1)} %dynamic-slice_bitcast_fusion.18, ...), kind=kOutput, calls=%fused_computation.91.clone.1 | convolution fusion | flops 612595712 | bytes 13600256 | tf_op jit(solution)/shard_map/transpose(jvp())/while/body/eval_jaxpr/ijh,jhp->ihp/dot_general | solution.py:40
  840.2 11.1 %fusion.235 = (f32[128,48]{0,1:T(8,128)S(1)}, f32[128,48]{0,1:T(8,128)S(1)}, f32[128,128]{1,0:T(8,128)S(1)}, f32[128,48]{0,1:T(8,128)S(1)}) fusion(f32[2,128,128,48]{2,1,3,0:T(8,128)} %get-tuple-element.2732, s32[]{:T(128)S(6)} %sub.274, f32[128,48]{0,1:T(8,128)S(1)} %dynamic-slice_bitcast_fusion.18, ...), kind=kOutput, calls=%fused_computation.91.clone.1 | convolution fusion | flops 612595712 | bytes 13600256 | tf_op jit(solution)/shard_map/transpose(jvp())/while/body/eval_jaxpr/ijh,jhp->ihp/dot_general | solution.py:40
  895.7 121.1 %all-reduce.2 = (f32[48]{0:T(128)S(1)}, f32[48]{0:T(128)S(1)}, f32[48]{0:T(128)S(1)}, f32[3072]{0:T(1024)S(1)}) all-reduce(f32[48]{0:T(128)S(1)} %get-tuple-element.1778, f32[48]{0:T(128)S(1)} %neg.49, f32[48]{0:T(128)S(1)} %copy-done.36, f32[3072]{0:T(1024)S(1)} %copy-done.32), channel_id=1, replica_groups=mesh['dp'=4,'seq'=32] {'seq'}, use_global_device_ids=true, to_apply=%region_27.28 | all-reduce | flops 3216 | bytes 25728 | tf_op jit(solution)/shard_map/psum | solution.py:170
  1016.8 13.9 %all-reduce.3 = (f32[48]{0:T(128)}, f32[48]{0:T(128)}, f32[48]{0:T(128)}, f32[3072]{0:T(1024)}) all-reduce(f32[48]{0:T(128)S(1)} %get-tuple-element.1923, f32[48]{0:T(128)S(1)} %get-tuple-element.1924, f32[48]{0:T(128)S(1)} %get-tuple-element.1925, f32[3072]{0:T(1024)S(1)} %get-tuple-element.1926), channel_id=1, replica_groups=mesh['dp'=4,'seq'=32] {'dp'}, use_global_device_ids=true, to_apply=%region_28.29 | all-reduce | flops 3216 | bytes 25728 | tf_op jit(solution)/shard_map/psum | solution.py:169
  (482 shorter events, 362.9 us)
Async XLA Ops:
  7.2 418.2 %copy-start = (bf16[1,256,1536]{2,1,0:T(8,128)(2,1)S(1)}, bf16[1,256,1536]{2,1,0:T(8,128)(2,1)}, u32[]{:S(2)}) copy-start(bf16[1,256,1536]{2,1,0:T(8,128)(2,1)} %param.31) | copy-start | bytes 2359300
  7.2 187.9 %all-gather.6.cloned.1.call-start = ((), (), s32[]{:S(2)}) async-start(), calls=%async_computation.3 | async-start | bytes 51904512 | tf_op jit(solution)/shard_map/all_gather | solution.py:12
  12.5 67.4 %copy-start.33 = (f32[48]{0:T(128)}, f32[48]{0:T(128)S(1)}, u32[]{:S(2)}) copy-start(f32[48]{0:T(128)S(1)} %neg.43) | copy-start | bytes 580
  33.8 518.9 %reduce-scatter.2.cloned.1.call-start = ((), (), s32[]{:S(2)}) async-start(), calls=%async_computation.1 | async-start | bytes 19464192 | tf_op jit(solution)/shard_map/reduce_scatter | solution.py:172
  33.9 45.9 %copy-start.12 = (f32[1,256,48]{2,1,0:T(8,128)}, f32[1,256,48]{2,1,0:T(8,128)S(1)}, u32[]{:S(2)}) copy-start(f32[1,256,48]{2,1,0:T(8,128)S(1)} %copy.179) | copy-start | bytes 147460
  49.7 5.5 copy-start.26
  49.7 30.2 %copy-start.29 = (f32[48]{0:T(128)S(1)}, f32[48]{0:T(128)}, u32[]{:S(2)}) copy-start(f32[48]{0:T(128)} %param.25) | copy-start | bytes 580
  330.8 4.9 copy-start.43
  413.7 7.7 copy-start.20
  433.2 280.7 %all-gather.8.cloned.1.call-start = ((), (), s32[]{:S(2)}) async-start(), calls=%async_computation.4 | async-start | bytes 51904512 | tf_op jit(solution)/shard_map/all_gather | solution.py:12
  446.1 6.4 copy-start.8
  446.1 6.4 copy-start.27
  452.5 10.8 %copy-start.10 = (f32[256,3072]{1,0:T(8,128)S(1)}, f32[256,3072]{1,0:T(8,128)}, u32[]{:S(2)}) copy-start(f32[256,3072]{1,0:T(8,128)} %reshape.1022) | copy-start | bytes 9437188
  452.5 10.8 %copy-start.11 = (bf16[1,256,3072]{2,1,0:T(8,128)(2,1)S(1)}, bf16[1,256,3072]{2,1,0:T(8,128)(2,1)}, u32[]{:S(2)}) copy-start(bf16[1,256,3072]{2,1,0:T(8,128)(2,1)} %param.21) | copy-start | bytes 4718596
  463.3 5.6 copy-start.9
  479.8 555.5 %all-reduce.6.cloned.1.call-start = ((), (), s32[]{:S(2)}) async-start(), calls=%async_computation.2 | async-start | bytes 1179648 | tf_op jit(solution)/shard_map/psum | solution.py:180
  797.9 84.8 %copy-start.13 = (f32[1,256,48]{2,1,0:T(8,128)S(1)}, f32[1,256,48]{2,1,0:T(8,128)}, u32[]{:S(2)}) copy-start(f32[1,256,48]{2,1,0:T(8,128)} %copy-done.12) | copy-start | bytes 147460
  797.9 84.8 %copy-start.30 = (f32[48]{0:T(128)S(1)}, f32[48]{0:T(128)}, u32[]{:S(2)}) copy-start(f32[48]{0:T(128)} %param.25) | copy-start | bytes 580
  797.9 84.8 %copy-start.34 = (f32[48]{0:T(128)S(1)}, f32[48]{0:T(128)}, u32[]{:S(2)}) copy-start(f32[48]{0:T(128)} %copy-done.33) | copy-start | bytes 580
  798.9 11.2 %copy-start.5 = (f32[2,48,64,128]{3,2,1,0:T(8,128)S(1)}, f32[2,48,64,128]{3,2,1,0:T(8,128)}, u32[]{:S(2)}) copy-start(f32[2,48,64,128]{3,2,1,0:T(8,128)} %get-tuple-element.2719) | copy-start | bytes 9437188 | tf_op jit(solution)/shard_map/transpose(jvp())/while
  821.9 9.6 copy-start.24
  821.9 9.9 copy-start.1
  821.9 9.9 copy-start.4
  831.8 5.5 copy-start.25
  840.2 11.2 %copy-start.5 = (f32[2,48,64,128]{3,2,1,0:T(8,128)S(1)}, f32[2,48,64,128]{3,2,1,0:T(8,128)}, u32[]{:S(2)}) copy-start(f32[2,48,64,128]{3,2,1,0:T(8,128)} %get-tuple-element.2719) | copy-start | bytes 9437188 | tf_op jit(solution)/shard_map/transpose(jvp())/while
  863.2 9.6 copy-start.24
  863.2 9.9 copy-start.1
  863.2 9.9 copy-start.4
  873.1 5.4 copy-start.25
  889.1 5.9 copy-start.15
  889.1 6.6 copy-start.32
  889.1 6.6 copy-start.36
  (34 other events, 101.2 us)
Sparse Core Ops, SparseCore 0:
  33.9 161.1 all-gather.5
  433.3 119.3 reduce-scatter.1
  555.8 158.0 all-gather.7
  716.2 40.1 all-reduce.5
